TPU v7x, 32 devices: a whole 2x2x4 slice. The times are simulated.
32 devices in a mesh: view: 4 (over y, core), row: 4 (over z), col: 2 (over x).
Axes of the slice: x: 2, y: 2, z: 4, core: 2. Of those that a mesh axis runs over, the one named last changes fastest.
Arguments:
- view_maps: bfloat16 [16, 16, 32, 768], P('view', 'row', 'col'), may hold values from -6 to 6
- gain_spatial: float32 [768], replicated, may hold values from 0.1 to 1.9
- spatial_query: bfloat16 [768, 768], replicated, may hold values from -8 to 8
- spatial_key: bfloat16 [768, 768], replicated, may hold values from -8 to 8
- spatial_value: bfloat16 [768, 768], replicated, may hold values from -0.21875 to 0.21875
- spatial_output: bfloat16 [768, 768], replicated, may hold values from -0.21875 to 0.21875
- gain_temporal: float32 [768], replicated, may hold values from 0.1 to 1.9
- temporal_query: bfloat16 [768, 768], replicated, may hold values from -8 to 8
- temporal_key: bfloat16 [768, 768], replicated, may hold values from -8 to 8
- temporal_value: bfloat16 [768, 768], replicated, may hold values from -0.21875 to 0.21875
- temporal_output: bfloat16 [768, 768], replicated, may hold values from -0.21875 to 0.21875
Outputs:
- refined: bfloat16 [16, 16, 32, 768], P('view', 'row', 'col')
All inputs are finite; a program needn't handle non-finite values.
Results may differ from a plain program's by a relative error of at most 0.012.
Values may be sent and summed in bfloat16 or wider, within the bound.
A program may use at most 64 MiB of HBM per device.

v0:
```python
import jax
import jax.numpy as jnp
from jax import lax
from jax.sharding import PartitionSpec as P

HEADS = 12
HEAD_DIM = 64
RADIUS = 3


epsilon = 1e-06
very_negative = -1e30


def padded(block, sides, width):
    for axis, dim in sides:
        count = lax.axis_size(axis)
        forward = [(i, i + 1) for i in range(count - 1)]
        backward = [(target, source) for source, target in forward]
        low = lax.ppermute(
            lax.slice_in_dim(block, block.shape[dim] - width, None, axis=dim), axis, forward
        )
        high = lax.ppermute(lax.slice_in_dim(block, 0, width, axis=dim), axis, backward)
        block = jnp.concatenate([low, block, high], axis=dim)
    return block


def rms_norm(tokens, gain_vector):
    values = tokens.astype(jnp.float32)
    scaled = values * lax.rsqrt(jnp.mean(values * values, axis=-1, keepdims=True) + epsilon)
    return (scaled * gain_vector).astype(jnp.bfloat16)


def project(tokens, weight_matrix):
    flat = tokens.reshape(-1, tokens.shape[-1])
    result = jnp.dot(flat, weight_matrix, preferred_element_type=jnp.float32)
    return result.reshape(tokens.shape[:-1] + (weight_matrix.shape[1],))


def grid_rows(count_rows, count_cols):
    return jnp.broadcast_to(
        jnp.arange(count_rows, dtype=jnp.int32)[:, None], (count_rows, count_cols)
    ).reshape(-1)


def grid_cols(count_rows, count_cols):
    return jnp.broadcast_to(
        jnp.arange(count_cols, dtype=jnp.int32)[None, :], (count_rows, count_cols)
    ).reshape(-1)


def neighbour(queries, keys_wide, values_wide, first_row, first_col, total_rows, total_cols):
    local_views, height, width, features = queries.shape
    wide_rows, wide_cols = (keys_wide.shape[1], keys_wide.shape[2])
    factor = HEAD_DIM ** (-0.5)
    query_rows = grid_rows(height, width)
    query_cols = grid_cols(height, width)
    key_rows = grid_rows(wide_rows, wide_cols)
    key_cols = grid_cols(wide_rows, wide_cols)
    row_gap = key_rows[None, :] - RADIUS - query_rows[:, None]
    col_gap = key_cols[None, :] - RADIUS - query_cols[:, None]
    in_band = (jnp.abs(row_gap) <= RADIUS) & (jnp.abs(col_gap) <= RADIUS)
    global_rows = first_row - RADIUS + key_rows
    global_cols = first_col - RADIUS + key_cols
    inside = (
        (global_rows >= 0)
        & (global_rows < total_rows)
        & (global_cols >= 0)
        & (global_cols < total_cols)
    )
    allowed = (in_band & inside[None, :])[None, :, :]

    def one_view(items):
        query_heads = items[0].reshape(height * width, HEADS, HEAD_DIM)
        key_heads = items[1].reshape(wide_rows * wide_cols, HEADS, HEAD_DIM)
        value_heads = items[2].reshape(wide_rows * wide_cols, HEADS, HEAD_DIM).astype(jnp.float32)
        scores = (
            jnp.einsum("qhe,khe->hqk", query_heads, key_heads, preferred_element_type=jnp.float32)
            * factor
        )
        scores = jnp.where(allowed, scores, very_negative)
        highest = jnp.max(scores, axis=-1, keepdims=True)
        weights = jnp.exp(scores - highest)
        weights = weights / jnp.sum(weights, axis=-1, keepdims=True)
        mixed = jnp.einsum("hqk,khe->qhe", weights, value_heads, precision=lax.Precision.HIGHEST)
        return mixed.reshape(height, width, features).astype(jnp.bfloat16)

    return lax.map(one_view, (queries, keys_wide, values_wide))


def body(
    view_maps,
    gain_spatial,
    spatial_query,
    spatial_key,
    spatial_value,
    spatial_output,
    gain_temporal,
    temporal_query,
    temporal_key,
    temporal_value,
    temporal_output,
):
    local_views, tile_rows, tile_cols = (view_maps.shape[0], view_maps.shape[1], view_maps.shape[2])
    total_rows = lax.axis_size("row") * tile_rows
    total_cols = lax.axis_size("col") * tile_cols
    first_row = lax.axis_index("row") * tile_rows
    first_col = lax.axis_index("col") * tile_cols
    normed = rms_norm(view_maps, gain_spatial)
    queries = project(normed, spatial_query).astype(jnp.bfloat16)
    keys = project(normed, spatial_key).astype(jnp.bfloat16)
    values = project(normed, spatial_value).astype(jnp.bfloat16)
    stacked = jnp.stack([keys, values], 0)
    widened = padded(stacked, (("row", 2), ("col", 3)), RADIUS)
    keys_wide = widened[0]
    values_wide = widened[1]
    attended = neighbour(
        queries, keys_wide, values_wide, first_row, first_col, total_rows, total_cols
    )
    middle = (view_maps.astype(jnp.float32) + project(attended, spatial_output)).astype(
        jnp.bfloat16
    )
    normed_time = rms_norm(middle, gain_temporal)
    factor = HEAD_DIM ** (-0.5)
    gathered = lax.all_to_all(normed_time, "view", split_axis=1, concat_axis=0, tiled=True)
    count_views = gathered.shape[0]
    count_tokens = gathered.shape[2]
    shape_heads = (count_views, count_tokens, HEADS, HEAD_DIM)
    query_heads = project(gathered, temporal_query).astype(jnp.bfloat16).reshape(shape_heads)
    key_heads = project(gathered, temporal_key).astype(jnp.bfloat16).reshape(shape_heads)
    value_heads = project(gathered, temporal_value).astype(jnp.bfloat16).reshape(shape_heads)
    scores = (
        jnp.einsum("qthe,kthe->qkth", query_heads, key_heads, preferred_element_type=jnp.float32)
        * factor
    )
    highest = jnp.max(scores, axis=1, keepdims=True)
    weights = jnp.exp(scores - highest)
    weights = weights / jnp.sum(weights, axis=1, keepdims=True)
    mixed = jnp.einsum("qkth,kthe->qthe", weights, value_heads.astype(jnp.float32))
    mixed_views = mixed.reshape(gathered.shape).astype(jnp.bfloat16)
    returned = lax.all_to_all(mixed_views, "view", split_axis=0, concat_axis=1, tiled=True)
    refined = (middle.astype(jnp.float32) + project(returned, temporal_output)).astype(jnp.bfloat16)
    return refined


def solution(mesh):
    return jax.shard_map(
        body,
        mesh=mesh,
        in_specs=(P("view", "row", "col", None), P(), P(), P(), P(), P(), P(), P(), P(), P(), P()),
        out_specs=P("view", "row", "col", None),
        check_vma=False,
    )
```

profile of v0, /device:TPU:0, one launch (start us, length us, event | category | flops | bytes accessed | tf_op | source)
XLA Modules:
  0.0 120.1 jit_solution(3309329166890147132)
XLA Ops:
  0.0 1.3 %fusion.38 = f32[4,4,16]{2,1,0:T(4,128)S(1)} fusion(bf16[4,4,16,768]{3,2,1,0:T(8,128)(2,1)} %param.13), kind=kLoop, calls=%fused_computation.57 | loop fusion | flops 589568 | bytes 394240 | tf_op jit(solution)/shard_map/reduce_sum | solution.py:30
  1.3 1.9 %fusion.28 = bf16[1,4,4,16,768]{4,3,2,1,0:T(8,128)(2,1)S(1)} fusion(bf16[768,768]{1,0:T(8,128)(2,1)} %param.16, bf16[4,4,16,768]{3,2,1,0:T(8,128)(2,1)} %param.13, f32[768]{0:T(1024)} %param.14, f32[4,4,16]{2,1,0:T(4,128)S(1)} %add_rsqrt_fusion.1), kind=kOutput, calls=%fused_computation.45 | convolution fusion | flops 302972928 | bytes 1970176 | tf_op jit(solution)/shard_map/dot_general | solution.py:36
  3.3 0.5 fusion.29
  3.8 1.1 fusion.46
  4.9 5.0 %collective-permute-start = (bf16[2,4,3,16,768]{4,3,2,1,0:T(8,128)(2,1)}, bf16[2,4,3,16,768]{4,3,2,1,0:T(8,128)(2,1)S(1)}, u32[]{:S(2)}, u32[]{:S(2)}) collective-permute-start(bf16[2,4,3,16,768]{4,3,2,1,0:T(8,128)(2,1)} %get-tuple-element.103), channel_id=1, source_target_pairs={{0,2},{2,4},{4,6},{1,3},{3,5},{5,7},{8,10},{10,12},{12,14},{9,11},... | collective-permute-start | bytes 1769480 | tf_op jit(solution)/shard_map/ppermute | solution.py:20
  9.9 1.3 %collective-permute-start.1 = (bf16[2,4,3,16,768]{4,3,2,1,0:T(8,128)(2,1)}, bf16[2,4,3,16,768]{4,3,2,1,0:T(8,128)(2,1)S(1)}, u32[]{:S(2)}, u32[]{:S(2)}) collective-permute-start(bf16[2,4,3,16,768]{4,3,2,1,0:T(8,128)(2,1)} %get-tuple-element.104), channel_id=1, source_target_pairs={{2,0},{4,2},{6,4},{3,1},{5,3},{7,5},{10,8},{12,10},{14,12},{11,9},... | collective-permute-start | bytes 1769480 | tf_op jit(solution)/shard_map/ppermute | solution.py:23
  11.3 0.6 reshape.311
  12.0 10.8 %collective-permute-done = bf16[2,4,3,16,768]{4,3,2,1,0:T(8,128)(2,1)S(1)} collective-permute-done((bf16[2,4,3,16,768]{4,3,2,1,0:T(8,128)(2,1)}, bf16[2,4,3,16,768]{4,3,2,1,0:T(8,128)(2,1)S(1)}, u32[]{:S(2)}, u32[]{:S(2)}) %collective-permute-start) | collective-permute-done | bytes 589856 | tf_op jit(solution)/shard_map/ppermute | solution.py:20
  22.8 4.0 %collective-permute-done.1 = bf16[2,4,3,16,768]{4,3,2,1,0:T(8,128)(2,1)S(1)} collective-permute-done((bf16[2,4,3,16,768]{4,3,2,1,0:T(8,128)(2,1)}, bf16[2,4,3,16,768]{4,3,2,1,0:T(8,128)(2,1)S(1)}, u32[]{:S(2)}, u32[]{:S(2)}) %collective-permute-start.1) | collective-permute-done | bytes 589856 | tf_op jit(solution)/shard_map/ppermute | solution.py:23
  26.8 1.3 %pad_maximum_fusion.5 = (bf16[2,4,10,3,768]{4,3,2,1,0:T(4,128)(2,1)}, bf16[2,4,10,3,768]{4,3,2,1,0:T(4,128)(2,1)}) fusion(bf16[2,4,3,16,768]{4,3,2,1,0:T(8,128)(2,1)S(1)} %collective-permute-done.1, bf16[2,4,3,16,768]{4,3,2,1,0:T(8,128)(2,1)S(1)} %collective-permute-done, bf16[1,4,4,16,768]{4,3,2,1,0:T(8,128)(2,1)S(1)} %fusion.29, ...), kind=kLoop, calls=%fused_computation.74 | loop fusion | flops 2949120 | bytes 2703360 | tf_op jit(solution)/shard_map/slice | solution.py:21
  28.1 4.2 %collective-permute-start.2 = (bf16[2,4,10,3,768]{4,3,2,1,0:T(4,128)(2,1)}, bf16[2,4,10,3,768]{4,3,2,1,0:T(4,128)(2,1)}, u32[]{:S(2)}, u32[]{:S(2)}) collective-permute-start(bf16[2,4,10,3,768]{4,3,2,1,0:T(4,128)(2,1)} %get-tuple-element.101), channel_id=1, source_target_pairs={{0,1},{2,3},{4,5},{6,7},{8,9},{10,11},{12,13},{14,15},{16,17},{18,... | collective-permute-start | bytes 1105928 | tf_op jit(solution)/shard_map/ppermute | solution.py:20
  32.3 1.3 %collective-permute-start.3 = (bf16[2,4,10,3,768]{4,3,2,1,0:T(4,128)(2,1)}, bf16[2,4,10,3,768]{4,3,2,1,0:T(4,128)(2,1)}, u32[]{:S(2)}, u32[]{:S(2)}) collective-permute-start(bf16[2,4,10,3,768]{4,3,2,1,0:T(4,128)(2,1)} %get-tuple-element.102), channel_id=1, source_target_pairs={{1,0},{3,2},{5,4},{7,6},{9,8},{11,10},{13,12},{15,14},{17,16},{19,... | collective-permute-start | bytes 1105928 | tf_op jit(solution)/shard_map/ppermute | solution.py:23
  33.8 0.6 broadcast_in_dim.36
  34.4 0.8 sub.85
  35.1 2.6 %convolution_convert_fusion.4 = bf16[4,4,16,768]{3,2,1,0:T(8,128)(2,1)} fusion(bf16[768,768]{1,0:T(8,128)(2,1)} %param.15, bf16[4,4,16,768]{3,2,1,0:T(8,128)(2,1)S(1)} %copy-done.1, f32[768]{0:T(1024)} %param.14, f32[4,4,16]{2,1,0:T(4,128)} %copy-done.5), kind=kOutput, calls=%fused_computation.42 | convolution fusion | flops 302972928 | bytes 1970176 | tf_op jit(solution)/shard_map/dot_general | solution.py:36
  37.7 3.4 %collective-permute-done.2 = bf16[2,4,10,3,768]{4,3,2,1,0:T(4,128)(2,1)} collective-permute-done((bf16[2,4,10,3,768]{4,3,2,1,0:T(4,128)(2,1)}, bf16[2,4,10,3,768]{4,3,2,1,0:T(4,128)(2,1)}, u32[]{:S(2)}, u32[]{:S(2)}) %collective-permute-start.2) | collective-permute-done | bytes 368672 | tf_op jit(solution)/shard_map/ppermute | solution.py:20
  41.1 4.9 %collective-permute-done.3 = bf16[2,4,10,3,768]{4,3,2,1,0:T(4,128)(2,1)} collective-permute-done((bf16[2,4,10,3,768]{4,3,2,1,0:T(4,128)(2,1)}, bf16[2,4,10,3,768]{4,3,2,1,0:T(4,128)(2,1)}, u32[]{:S(2)}, u32[]{:S(2)}) %collective-permute-start.3) | collective-permute-done | bytes 368672 | tf_op jit(solution)/shard_map/ppermute | solution.py:23
  46.0 3.1 %pad_maximum_fusion = bf16[2,4,10,22,768]{4,3,2,1,0:T(8,128)(2,1)S(1)} fusion(bf16[2,4,10,3,768]{4,3,2,1,0:T(4,128)(2,1)} %collective-permute-done.3, bf16[2,4,3,16,768]{4,3,2,1,0:T(8,128)(2,1)S(1)} %collective-permute-done.1, bf16[1,4,4,16,768]{4,3,2,1,0:T(8,128)(2,1)S(1)} %fusion.29, bf16[1,4,4,16,768]{4,3,2,1,0:T(8,128)(2,1)S(1)} %fusion.28, ...), kind=kLoop, calls=%fused_computation.22 | loop fusion | flops 16220160 | bytes 5406720 | tf_op jit(solution)/shard_map/concatenate | solution.py:24
  49.1 1.8 %slice_bitcast_fusion = (bf16[4,10,22,768]{3,2,1,0:T(8,128)(2,1)}, bf16[4,10,22,768]{3,2,1,0:T(8,128)(2,1)}) fusion(bf16[2,4,10,22,768]{4,3,2,1,0:T(8,128)(2,1)S(1)} %pad_maximum_fusion), kind=kLoop, calls=%fused_computation.29 | loop fusion | bytes 5406720 | tf_op jit(solution)/shard_map/squeeze | solution.py:115
  50.9 26.6 %while.11 = (s32[]{:T(128)}, bf16[4,4,16,768]{3,2,1,0:T(8,128)(2,1)}, bf16[4,10,22,768]{3,2,1,0:T(8,128)(2,1)}, bf16[4,4,16,768]{3,2,1,0:T(8,128)(2,1)}, bf16[4,...) while((s32[]{:T(128)}, ...), condition=%wide.region_4.5_spmd.clone, body=%wide.region_1.4_spmd.clone.sunk | while | flops 152731136 | bytes 6633009 | solution.py:88
  50.9 1.1 constant_dynamic-slice_fusion.5
  52.1 0.5 reshape.326
  52.7 0.9 constant_dynamic-slice_fusion.6
  53.8 0.6 fusion.73
  54.8 0.5 reshape.328
  55.3 1.1 fusion.75
  56.9 0.7 constant_dynamic-update-slice_fusion.2
  57.6 1.1 constant_dynamic-slice_fusion.5
  58.7 0.5 reshape.326
  59.4 0.9 constant_dynamic-slice_fusion.6
  60.5 0.6 fusion.73
  61.1 0.3 fusion.74
  61.4 0.5 reshape.328
  62.0 1.2 fusion.75
  63.6 0.7 constant_dynamic-update-slice_fusion.2
  64.2 1.1 constant_dynamic-slice_fusion.5
  65.4 0.5 reshape.326
  66.0 0.9 constant_dynamic-slice_fusion.6
  67.1 0.6 fusion.73
  68.1 0.5 reshape.328
  68.7 1.2 fusion.75
  70.2 0.7 constant_dynamic-update-slice_fusion.2
  70.9 1.1 constant_dynamic-slice_fusion.5
  72.0 0.5 reshape.326
  72.7 0.9 constant_dynamic-slice_fusion.6
  73.8 0.6 fusion.73
  74.8 0.5 reshape.328
  75.3 1.2 fusion.75
  76.9 0.7 constant_dynamic-update-slice_fusion.2
  77.6 1.7 %multiply_reduce_fusion = (f32[4,4,16]{2,1,0:T(4,128)S(1)}, f32[4,4,16,768]{3,2,1,0:T(8,128)S(1)}) fusion(bf16[4,4,16,768]{3,2,1,0:T(8,128)(2,1)} %get-tuple-element.37, bf16[768,768]{1,0:T(8,128)(2,1)S(1)} %copy-done, bf16[4,4,16,768]{3,2,1,0:T(8,128)(2,1)} %param.13), kind=kOutput, calls=%fused_computation.68 | convolution fusion | flops 303169280 | bytes 2753536 | tf_op jit(solution)/shard_map/dot_general | solution.py:36
  79.5 10.2 %all_to_all.30 = bf16[4,4,16,768]{3,2,0,1:T(8,128)(2,1)S(1)} all-to-all(bf16[4,4,16,768]{3,2,0,1:T(8,128)(2,1)S(1)} %copy.34), channel_id=1, replica_groups=mesh['view'=4,'row'=4,'col'=2] {'view'}, dimensions={1} | all-to-all | bytes 786432 | tf_op jit(solution)/shard_map/all_to_all | solution.py:125
  89.7 1.2 %convolution_convert_fusion.2 = bf16[16,16,768]{2,1,0:T(8,128)(2,1)} fusion(bf16[16,16,768]{2,1,0:T(8,128)(2,1)S(1)} %bitcast.84, bf16[768,768]{1,0:T(8,128)(2,1)S(1)} %copy-done.2), kind=kOutput, calls=%fused_computation.40 | convolution fusion | flops 302186496 | bytes 1966080 | tf_op jit(solution)/shard_map/dot_general | solution.py:36
  90.9 1.7 %reshape.309 = bf16[16,16,12,64]{3,2,1,0:T(8,128)(2,1)S(1)} reshape(bf16[16,16,768]{2,1,0:T(8,128)(2,1)} %convolution_convert_fusion.2) | data formatting | bytes 786432 | tf_op jit(solution)/shard_map/reshape | solution.py:130
  92.5 2.5 %convolution_convert_fusion.1 = bf16[16,16,768]{2,1,0:T(8,128)(2,1)} fusion(bf16[16,16,768]{2,1,0:T(8,128)(2,1)S(1)} %bitcast.85, bf16[768,768]{1,0:T(8,128)(2,1)} %param.20), kind=kOutput, calls=%fused_computation.39 | convolution fusion | flops 302186496 | bytes 1966080 | tf_op jit(solution)/shard_map/dot_general | solution.py:36
  95.0 2.4 %reshape.310 = bf16[16,16,12,64]{3,2,1,0:T(8,128)(2,1)} reshape(bf16[16,16,768]{2,1,0:T(8,128)(2,1)} %convolution_convert_fusion.1) | data formatting | bytes 786432 | tf_op jit(solution)/shard_map/reshape | solution.py:129
  97.5 2.5 %convolution_convert_fusion.3 = bf16[16,16,768]{2,1,0:T(8,128)(2,1)} fusion(bf16[16,16,768]{2,1,0:T(8,128)(2,1)S(1)} %bitcast.86, bf16[768,768]{1,0:T(8,128)(2,1)} %param.22), kind=kOutput, calls=%fused_computation.41 | convolution fusion | flops 302186496 | bytes 1966080 | tf_op jit(solution)/shard_map/dot_general | solution.py:36
  100.0 2.5 %reshape.308 = bf16[16,16,12,64]{3,2,1,0:T(8,128)(2,1)} reshape(bf16[16,16,768]{2,1,0:T(8,128)(2,1)} %convolution_convert_fusion.3) | data formatting | bytes 786432 | tf_op jit(solution)/shard_map/reshape | solution.py:131
  102.4 2.4 %bitcast_reduce_fusion = (f32[16,16,12]{0,2,1:T(8,128)S(1)}, f32[16,12,16,16]{3,2,1,0:T(8,128)S(1)}) fusion(bf16[16,16,12,64]{3,2,1,0:T(8,128)(2,1)} %reshape.310, bf16[16,16,12,64]{3,2,1,0:T(8,128)(2,1)S(1)} %reshape.309), kind=kOutput, calls=%fused_computation.24 | convolution fusion | flops 6386688 | bytes 995328 | tf_op jit(solution)/shard_map/qthe,kthe->qkth/dot_general | solution.py:133
  104.8 0.6 fusion.21
  105.4 0.7 copy-done.3
  106.0 0.8 fusion.22
  107.1 0.6 convert_element_type.89
  107.7 9.8 %all_to_all.31 = bf16[16,1,16,768]{3,2,1,0:T(8,128)(2,1)S(1)} all-to-all(bf16[16,1,16,768]{3,2,1,0:T(8,128)(2,1)S(1)} %bitcast.87), channel_id=1, replica_groups=mesh['view'=4,'row'=4,'col'=2] {'view'}, dimensions={0} | all-to-all | bytes 786432 | tf_op jit(solution)/shard_map/all_to_all | solution.py:141
  117.6 2.5 %fusion.27 = bf16[4,4,16,768]{3,2,1,0:T(8,128)(2,1)} fusion(f32[4,4,16,768]{3,2,1,0:T(8,128)S(1)} %get-tuple-element.106, bf16[768,768]{1,0:T(8,128)(2,1)} %param.23, bf16[4,4,1,16,768]{4,3,1,0,2:T(8,128)(2,1)S(1)} %bitcast.88), kind=kOutput, calls=%fused_computation.38 | convolution fusion | flops 302383104 | bytes 2752512 | tf_op jit(solution)/shard_map/dot_general | solution.py:36
  (49 shorter events, 4.6 us)
Async XLA Ops:
  0.0 77.6 %copy-start = (bf16[768,768]{1,0:T(8,128)(2,1)S(1)}, bf16[768,768]{1,0:T(8,128)(2,1)}, u32[]{:S(2)}) copy-start(bf16[768,768]{1,0:T(8,128)(2,1)} %param.18) | copy-start | bytes 3538948
  0.0 3.3 %copy-start.1 = (bf16[4,4,16,768]{3,2,1,0:T(8,128)(2,1)S(1)}, bf16[4,4,16,768]{3,2,1,0:T(8,128)(2,1)}, u32[]{:S(2)}) copy-start(bf16[4,4,16,768]{3,2,1,0:T(8,128)(2,1)} %param.13) | copy-start | bytes 1179652
  0.0 3.3 %copy-start.8 = (f32[768]{0:T(1024)S(1)}, f32[768]{0:T(1024)}, u32[]{:S(2)}) copy-start(f32[768]{0:T(1024)} %param.14) | copy-start | bytes 9220
  0.0 3.3 %copy-start.7 = (bf16[768,768]{1,0:T(8,128)(2,1)S(1)}, bf16[768,768]{1,0:T(8,128)(2,1)}, u32[]{:S(2)}) copy-start(bf16[768,768]{1,0:T(8,128)(2,1)} %param.17) | copy-start | bytes 3538948
  1.3 2.5 %copy-start.5 = (f32[4,4,16]{2,1,0:T(4,128)}, f32[4,4,16]{2,1,0:T(4,128)S(1)}, u32[]{:S(2)}) copy-start(f32[4,4,16]{2,1,0:T(4,128)S(1)} %add_rsqrt_fusion.1) | copy-start | bytes 3076
  4.9 17.8 %collective-permute-start = (bf16[2,4,3,16,768]{4,3,2,1,0:T(8,128)(2,1)}, bf16[2,4,3,16,768]{4,3,2,1,0:T(8,128)(2,1)S(1)}, u32[]{:S(2)}, u32[]{:S(2)}) collective-permute-start(bf16[2,4,3,16,768]{4,3,2,1,0:T(8,128)(2,1)} %get-tuple-element.103), channel_id=1, source_target_pairs={{0,2},{2,4},{4,6},{1,3},{3,5},{5,7},{8,10},{10,12},{12,14},{9,11},... | collective-permute-start | bytes 1769480 | tf_op jit(solution)/shard_map/ppermute | solution.py:20
  9.9 16.9 %collective-permute-start.1 = (bf16[2,4,3,16,768]{4,3,2,1,0:T(8,128)(2,1)}, bf16[2,4,3,16,768]{4,3,2,1,0:T(8,128)(2,1)S(1)}, u32[]{:S(2)}, u32[]{:S(2)}) collective-permute-start(bf16[2,4,3,16,768]{4,3,2,1,0:T(8,128)(2,1)} %get-tuple-element.104), channel_id=1, source_target_pairs={{2,0},{4,2},{6,4},{3,1},{5,3},{7,5},{10,8},{12,10},{14,12},{11,9},... | collective-permute-start | bytes 1769480 | tf_op jit(solution)/shard_map/ppermute | solution.py:23
  28.1 13.0 %collective-permute-start.2 = (bf16[2,4,10,3,768]{4,3,2,1,0:T(4,128)(2,1)}, bf16[2,4,10,3,768]{4,3,2,1,0:T(4,128)(2,1)}, u32[]{:S(2)}, u32[]{:S(2)}) collective-permute-start(bf16[2,4,10,3,768]{4,3,2,1,0:T(4,128)(2,1)} %get-tuple-element.101), channel_id=1, source_target_pairs={{0,1},{2,3},{4,5},{6,7},{8,9},{10,11},{12,13},{14,15},{16,17},{18,... | collective-permute-start | bytes 1105928 | tf_op jit(solution)/shard_map/ppermute | solution.py:20
  32.3 13.7 %collective-permute-start.3 = (bf16[2,4,10,3,768]{4,3,2,1,0:T(4,128)(2,1)}, bf16[2,4,10,3,768]{4,3,2,1,0:T(4,128)(2,1)}, u32[]{:S(2)}, u32[]{:S(2)}) collective-permute-start(bf16[2,4,10,3,768]{4,3,2,1,0:T(4,128)(2,1)} %get-tuple-element.102), channel_id=1, source_target_pairs={{1,0},{3,2},{5,4},{7,6},{9,8},{11,10},{13,12},{15,14},{17,16},{19,... | collective-permute-start | bytes 1105928 | tf_op jit(solution)/shard_map/ppermute | solution.py:23
  49.1 1.8 %copy-start.4 = (pred[220]{0:T(512)(128)(4,1)S(1)}, pred[220]{0:T(512)(128)(4,1)}, u32[]{:S(2)}) copy-start(pred[220]{0:T(512)(128)(4,1)} %reshape.311) | copy-start | bytes 664
  77.6 1.7 %copy-start.6 = (f32[768]{0:T(1024)S(1)}, f32[768]{0:T(1024)}, u32[]{:S(2)}) copy-start(f32[768]{0:T(1024)} %param.19) | copy-start | bytes 9220
  79.2 10.4 %copy-start.2 = (bf16[768,768]{1,0:T(8,128)(2,1)S(1)}, bf16[768,768]{1,0:T(8,128)(2,1)}, u32[]{:S(2)}) copy-start(bf16[768,768]{1,0:T(8,128)(2,1)} %param.21) | copy-start | bytes 3538948
  104.8 1.2 %copy-start.3 = (bf16[16,16,12,64]{3,2,1,0:T(8,128)(2,1)S(1)}, bf16[16,16,12,64]{3,2,1,0:T(8,128)(2,1)}, u32[]{:S(2)}) copy-start(bf16[16,16,12,64]{3,2,1,0:T(8,128)(2,1)} %reshape.308) | copy-start | bytes 1179652
where the time goes:
time: 121 us; the launch traced here: 120 us
  local copies, waits for them, and re-layouts  29.6 us (24%)
  matrix products  25.8 us (21%)
  waiting for transfers between devices  23.1 us (19%)
  blocking collectives  20 us (17%)
  starting transfers between devices  11.7 us (10%)
  other arithmetic  9.35 us (8%)
    dot_general x8, matrix products, project(): result = jnp.dot(flat, weight_matrix, preferred_element_type=jnp.float32)  15.4 us
    ppermute x2, waiting for transfers between devices, padded(): lax.ppermute(lax.slice_in_dim(block, block.shape[dim] - width, None, axis...  14.2 us
    all_to_all x1, blocking collectives, body(): lax.all_to_all(normed_time, 'view', split_axis=1, concat_axis=0, tiled=True)  10.2 us
    all_to_all x1, blocking collectives, body(): lax.all_to_all(mixed_views, 'view', split_axis=0, concat_axis=1, tiled=True)  9.84 us
    ppermute x2, starting transfers between devices, padded(): lax.ppermute(lax.slice_in_dim(block, block.shape[dim] - width, None, axis...  9.14 us
    ppermute x2, waiting for transfers between devices, padded(): lax.ppermute(lax.slice_in_dim(block, 0, width, axis=dim), axis, backward)  8.93 us
    dynamic_slice x8, local copies, waits for them, and re-layouts, neighbour(): return lax.map(one_view, (queries, keys_wide, values_wide))  8.21 us
    dot_general x4, matrix products, one_view(): jnp.einsum('hqk,khe->qhe', weights, value_heads, precision=lax.Precision....  4.6 us
  transfers between devices with their start and end apart: 4, of which 4 were waited for; matrix products, arithmetic and copies ran while one was open for 4% of the time, Pallas kernels for 0%

commit v1 on v0

v1 whole, which is shorter than its diff:
```python
import functools

import jax
import jax.numpy as jnp
from jax import lax
from jax.experimental import pallas as pl
from jax.experimental.pallas import tpu as pltpu
from jax.sharding import PartitionSpec as P

HEAD_DIM = 64
RADIUS = 3
LANES = 256
GROUP = LANES // HEAD_DIM
ROWS = 16
COLS = 8

epsilon = 1e-06
very_negative = -1e30
DIRECTIONS = [(dz, dx) for dz in (-1, 0, 1) for dx in (-1, 0, 1) if dz or dx]


def rms_norm(tokens, gain):
    values = tokens.astype(jnp.float32)
    mean = jnp.mean(values * values, axis=-1, keepdims=True)
    return (values * lax.rsqrt(mean + epsilon) * gain).astype(jnp.bfloat16)


def dot(a, b):
    return jnp.dot(a, b, preferred_element_type=jnp.float32)


def dot_t(a, b):
    return lax.dot_general(a, b, (((1,), (1,)), ((), ())), preferred_element_type=jnp.float32)


def head_masks(rows):
    lane = lax.broadcasted_iota(jnp.int32, (rows, LANES), 1)
    return [(lane >= h * HEAD_DIM) & (lane < (h + 1) * HEAD_DIM) for h in range(GROUP)]


def attend(query, key, value, bias, masks):
    rows = query.shape[0]
    zero = jnp.zeros_like(query)
    stacked = jnp.concatenate([jnp.where(m, query, zero) for m in masks], axis=0)
    scores = dot_t(stacked, key)
    scores = (scores.reshape(GROUP, rows, -1) + bias[None]).reshape(GROUP * rows, -1)
    highest = jnp.max(scores, axis=-1, keepdims=True)
    weights = jnp.exp(scores - highest)
    total = jnp.sum(weights, axis=-1, keepdims=True)
    mixed = dot(weights.astype(jnp.bfloat16), value) * (1.0 / total)
    result = mixed[:rows]
    for h in range(1, GROUP):
        result = jnp.where(masks[h], mixed[h * rows : (h + 1) * rows], result)
    return result


def kernel(
    height, width, side_rows, sizes, x_hbm, gain_s, gain_t, *refs
):
    nv, nz, nx = sizes
    weights_hbm, refs = refs[:8], refs[8:]
    out_ref, wide, sides, w, qbuf, mid, held, normed, kbuf, vbuf, back = refs[:11]
    x_sem, w_sem, hs, hr, ms, mr, bs, br = refs[11:]
    views, own, depth = x_hbm.shape
    share = own // nv
    halo = RADIUS * width
    main = own + 2 * halo
    me, z, x = lax.axis_index("view"), lax.axis_index("row"), lax.axis_index("col")

    x_copy = pltpu.make_async_copy(x_hbm, wide.at[:, pl.ds(halo, own)], x_sem)
    x_copy.start()
    w_copies = [
        pltpu.make_async_copy(weights_hbm[i], w.at[i], w_sem.at[i]) for i in range(8)
    ]
    for copy in w_copies:
        copy.start()

    def there(dz, dx):
        ok = None
        for place, step, count in ((z, dz, nz), (x, dx, nx)):
            if step:
                one = place > 0 if step < 0 else place < count - 1
                ok = one if ok is None else ok & one
        return ok

    def peer(j):
        if nv % 2:
            return lax.rem(me + 1 + j, nv)
        chip, core = me // 2, lax.rem(me, 2)
        k, flip = j // 2 + 1, j % 2
        if j < nv - 2:
            return lax.rem(chip + k, nv // 2) * 2 + (core if flip == 0 else 1 - core)
        return chip * 2 + 1 - core if j == nv - 2 else me

    wide[:, :halo] = jnp.zeros((views, halo, depth), wide.dtype)
    wide[:, halo + own :] = jnp.zeros((views, wide.shape[1] - halo - own, depth), wide.dtype)

    barrier = pltpu.get_barrier_semaphore()
    expected = jnp.int32(nv - 1)
    for dz, dx in DIRECTIONS:
        ok = there(dz, dx)
        expected = expected + ok.astype(jnp.int32)

        @pl.when(ok)
        def _():
            pl.semaphore_signal(
                barrier, inc=1, device_id={"row": z + dz, "col": x + dx},
                device_id_type=pl.DeviceIdType.MESH,
            )

    for j in range(nv - 1):
        pl.semaphore_signal(
            barrier, inc=1, device_id={"view": peer(j)}, device_id_type=pl.DeviceIdType.MESH
        )

    x_copy.wait()
    row = lax.broadcasted_iota(jnp.int32, (2 * side_rows, own), 0)
    cell = lax.broadcasted_iota(jnp.int32, (2 * side_rows, own), 1)
    right = row >= side_rows
    t = jnp.where(right, row - side_rows, row)
    wanted = (t // RADIUS) * width + lax.rem(t, RADIUS) + jnp.where(right, width - RADIUS, 0)
    pick = ((cell == wanted) & (t < RADIUS * height)).astype(jnp.bfloat16)
    for v in range(views):
        packed = dot(pick, wide[v, pl.ds(halo, own)]).astype(jnp.bfloat16)
        sides[v] = packed.reshape(2, side_rows, depth)

    pl.semaphore_wait(barrier, expected)

    def halo_copy(k, v):
        dz, dx = DIRECTIONS[k]
        if dx == 0:
            start = own - halo if dz > 0 else 0
            source = x_hbm.at[v, pl.ds(start, halo)]
            target = wide.at[v, pl.ds(0 if dz > 0 else halo + own, halo)]
        else:
            source = sides.at[v, 0 if dx < 0 else 1]
            block = (0 if dx > 0 else 3) + 1 - dz
            target = wide.at[v, pl.ds(main + block * side_rows, side_rows)]
        return pltpu.make_async_remote_copy(
            src_ref=source, dst_ref=target, send_sem=hs.at[k, v], recv_sem=hr.at[k, v],
            device_id={"row": z + dz, "col": x + dx}, device_id_type=pl.DeviceIdType.MESH,
        )

    for v in range(views):
        for k, (dz, dx) in enumerate(DIRECTIONS):

            @pl.when(there(dz, dx))
            def _():
                halo_copy(k, v).start()

    shape = (own, wide.shape[1])
    query = lax.broadcasted_iota(jnp.int32, shape, 0)
    key = lax.broadcasted_iota(jnp.int32, shape, 1)
    query_row, query_col = query // width, lax.rem(query, width)
    at_side = key >= main
    side_key = key - main
    block, t = side_key // side_rows, lax.rem(side_key, side_rows)
    vertical, on_right = lax.rem(block, 3), block // 3
    key_row = jnp.where(at_side, (vertical - 1) * height + t // RADIUS, key // width - RADIUS)
    key_col = jnp.where(
        at_side, jnp.where(on_right > 0, width, -RADIUS) + lax.rem(t, RADIUS), lax.rem(key, width)
    )
    map_row, map_col = z * height + key_row, x * width + key_col
    seen = (
        (jnp.abs(key_row - query_row) <= RADIUS)
        & (jnp.abs(key_col - query_col) <= RADIUS)
        & (map_row >= 0) & (map_row < nz * height)
        & (map_col >= 0) & (map_col < nx * width)
        & (jnp.logical_not(at_side) | (t < RADIUS * height))
    )
    bias = jnp.where(seen, 0.0, very_negative).astype(jnp.float32)
    scale = HEAD_DIM ** -0.5
    gain = gain_s[...]
    groups = depth // LANES

    own_normed = rms_norm(wide[:, pl.ds(halo, own)].reshape(views * own, depth), gain)
    w_copies[0].wait()
    qbuf[...] = (
        (dot(own_normed, w[0]).astype(jnp.bfloat16) * scale)
        .astype(jnp.bfloat16).reshape(views, own, depth)
    )
    for i in (1, 2, 3):
        w_copies[i].wait()

    def mid_copy(v, target, slot):
        return pltpu.make_async_remote_copy(
            src_ref=mid.at[v, target], dst_ref=held.at[slot, v],
            send_sem=ms.at[target, v], recv_sem=mr.at[slot, v],
            device_id={"view": target}, device_id_type=pl.DeviceIdType.MESH,
        )

    masks = head_masks(own)

    def one_view(v, carry):
        for k, (dz, dx) in enumerate(DIRECTIONS):

            @pl.when(there(-dz, -dx))
            def _():
                halo_copy(k, v).wait_recv()

        tokens = rms_norm(wide[v], gain)
        keys = dot(tokens, w[1]).astype(jnp.bfloat16)
        values = dot(tokens, w[2]).astype(jnp.bfloat16)
        queries = qbuf[v]
        parts = []
        for g in range(groups):
            lanes = slice(g * LANES, (g + 1) * LANES)
            parts.append(
                attend(queries[:, lanes], keys[:, lanes], values[:, lanes], bias, masks)
                .astype(jnp.bfloat16)
            )
        attended = jnp.concatenate(parts, axis=1)
        added = wide[v, pl.ds(halo, own)].astype(jnp.float32) + dot(attended, w[3])
        mid[v] = added.astype(jnp.bfloat16).reshape(nv, share, depth)
        for j in range(nv - 1):
            mid_copy(v, peer(j), me).start()
        held[me, v] = mid[v, me]
        return carry

    lax.fori_loop(0, views, one_view, 0)

    for j in range(nv - 1):
        for v in range(views):
            mid_copy(v, peer(j), peer(j)).wait_recv()
    tokens = rms_norm(held[...].reshape(nv * views * share, depth), gain_t[...])
    normed[...] = tokens.reshape(nv, views * share, depth)
    for i in range(4, 8):
        w_copies[i].wait()
    all_views = nv * views
    cuts = share // COLS

    def cut(array, h):
        part = array.reshape(-1, share, array.shape[-1])[:, h * COLS : (h + 1) * COLS]
        return part.reshape(-1, array.shape[-1])

    keys = dot(tokens, w[5])
    values = dot(tokens, w[6])
    for h in range(cuts):
        kbuf[h] = cut(keys, h).astype(jnp.bfloat16)
        vbuf[h] = cut(values, h).astype(jnp.bfloat16)

    def back_copy(target, slot):
        return pltpu.make_async_remote_copy(
            src_ref=back.at[target], dst_ref=out_ref.at[:, slot],
            send_sem=bs.at[target], recv_sem=br.at[slot],
            device_id={"view": target}, device_id_type=pl.DeviceIdType.MESH,
        )

    step = 1 if nv % 2 else 2
    shape = (step * views * COLS, all_views * COLS)
    query = lax.broadcasted_iota(jnp.int32, shape, 0)
    key = lax.broadcasted_iota(jnp.int32, shape, 1)
    same = jnp.where(lax.rem(query, COLS) == lax.rem(key, COLS), 0.0, very_negative)
    same = same.astype(jnp.float32)
    masks = head_masks(shape[0])
    for first in range(0, nv, step):
        targets = [peer(j) for j in range(first, first + step)]
        chunk = jnp.concatenate([normed[p] for p in targets], axis=0)
        queries = dot(chunk, w[4]).astype(jnp.bfloat16).astype(jnp.float32) * scale
        cut_parts = []
        for h in range(cuts):
            query_cut = cut(queries, h).astype(jnp.bfloat16)
            parts = []
            for g in range(groups):
                lanes = slice(g * LANES, (g + 1) * LANES)
                parts.append(
                    attend(query_cut[:, lanes], kbuf[h, :, lanes], vbuf[h, :, lanes], same, masks)
                )
            cut_parts.append(jnp.concatenate(parts, axis=1).reshape(-1, COLS, depth))
        attended = jnp.concatenate(cut_parts, axis=1).reshape(-1, depth).astype(jnp.bfloat16)
        product = dot(attended, w[7])
        for i, p in enumerate(targets):
            rows = slice(i * views * share, (i + 1) * views * share)
            refined = held[p].reshape(views * share, depth).astype(jnp.float32) + product[rows]
            refined = refined.astype(jnp.bfloat16).reshape(views, share, depth)
            if first + i == nv - 1:
                out_ref[:, p] = refined
            else:
                back[p] = refined
                back_copy(p, me).start()

    for j in range(nv - 1):
        back_copy(peer(j), peer(j)).wait_recv()
    for j in range(nv - 1):
        back_copy(peer(j), me).wait_send()
        for v in range(views):
            mid_copy(v, peer(j), me).wait_send()
    for v in range(views):
        for k, (dz, dx) in enumerate(DIRECTIONS):

            @pl.when(there(dz, dx))
            def _():
                halo_copy(k, v).wait_send()


def body(sizes, view_maps, gain_spatial, *rest):
    spatial, gain_temporal, temporal = rest[:4], rest[4], rest[5:]
    views, height, width, depth = view_maps.shape
    nv = sizes[0]
    own = height * width
    share = own // nv
    side_rows = -(-RADIUS * height // ROWS) * ROWS
    wide = own + 2 * RADIUS * width + 6 * side_rows
    assert own % nv == 0 and share % ROWS == 0 and width % ROWS == 0
    assert height >= RADIUS and width >= RADIUS and depth % LANES == 0
    half = jnp.bfloat16
    hbm = pl.BlockSpec(memory_space=pl.ANY)
    vmem = pl.BlockSpec(memory_space=pltpu.VMEM)
    dma = pltpu.SemaphoreType.DMA
    tokens = nv * views * share
    products = 2 * depth * depth * (8 * views * own + 2 * views * (wide - own))
    result = pl.pallas_call(
        functools.partial(kernel, height, width, side_rows, sizes),
        out_shape=jax.ShapeDtypeStruct((views, nv, share, depth), half),
        in_specs=[hbm, vmem, vmem] + [hbm] * 8,
        out_specs=vmem,
        scratch_shapes=[
            pltpu.VMEM((views, wide, depth), half),
            pltpu.VMEM((views, 2, side_rows, depth), half),
            pltpu.VMEM((8, depth, depth), half),
            pltpu.VMEM((views, own, depth), half),
            pltpu.VMEM((views, nv, share, depth), half),
            pltpu.VMEM((nv, views, share, depth), half),
            pltpu.VMEM((nv, views * share, depth), half),
            pltpu.VMEM((share // COLS, tokens // (share // COLS), depth), half),
            pltpu.VMEM((share // COLS, tokens // (share // COLS), depth), half),
            pltpu.VMEM((nv, views, share, depth), half),
            dma(()),
            dma((8,)),
            dma((len(DIRECTIONS), views)),
            dma((len(DIRECTIONS), views)),
            dma((nv, views)),
            dma((nv, views)),
            dma((nv,)),
            dma((nv,)),
        ],
        compiler_params=pltpu.CompilerParams(
            collective_id=0, has_side_effects=True, vmem_limit_bytes=48 * 1024 * 1024
        ),
        cost_estimate=pl.CostEstimate(
            flops=products, bytes_accessed=16 * depth * depth, transcendentals=0
        ),
    )(
        view_maps.reshape(views, own, depth),
        gain_spatial.reshape(1, depth),
        gain_temporal.reshape(1, depth),
        *spatial,
        *temporal,
    )
    return result.reshape(view_maps.shape)


def solution(mesh):
    sizes = (mesh.shape["view"], mesh.shape["row"], mesh.shape["col"])
    maps = P("view", "row", "col", None)
    return jax.shard_map(
        functools.partial(body, sizes),
        mesh=mesh,
        in_specs=(maps,) + (P(),) * 10,
        out_specs=maps,
        check_vma=False,
    )
```

time: 121 us -> 37 us (0.31)
  Pallas kernels: 0 us -> 28.5 us
  matrix products: 25.8 us -> 0 us
  waiting for transfers between devices: 23.1 us -> 0 us
  local copies, waits for them, and re-layouts: 29.6 us -> 8.2 us
  blocking collectives: 20 us -> 0 us
  starting transfers between devices: 11.7 us -> 0 us
  other arithmetic: 9.35 us -> 0 us
    pallas_call x0 -> x1, Pallas kernels: none -> 28.5 us  [body(): pl.pallas_call(functools.partial(kernel, height, width, side_rows, sizes)...]
    dot_general x18 -> x0, matrix products: 25.8 us -> none  [the longest x8 15.4 us: project(): result = jnp.dot(flat, weight_matrix, preferred_element_type=jnp.float32)]
    ppermute x4 -> x0, waiting for transfers between devices: 23.1 us -> none  [the longest x2 14.2 us: padded(): lax.ppermute(lax.slice_in_dim(block, block.shape[dim] - width, None, axis...]
    all_to_all x2 -> x0, blocking collectives: 20 us -> none  [the longest x1 10.2 us: body(): lax.all_to_all(normed_time, 'view', split_axis=1, concat_axis=0, tiled=True)]
    ppermute x4 -> x0, starting transfers between devices: 11.7 us -> none  [the longest x2 9.14 us: padded(): lax.ppermute(lax.slice_in_dim(block, block.shape[dim] - width, None, axis...]
    reshape x15 -> x2, local copies, waits for them, and re-layouts: 11.5 us -> 1.38 us  [the longest x1 0.69 us: body(): gain_spatial.reshape(1, depth)]
    dynamic_slice x8 -> x0, local copies, waits for them, and re-layouts: 8.21 us -> none  [neighbour(): return lax.map(one_view, (queries, keys_wide, values_wide))]
    unnamed x18 -> x11, local copies, waits for them, and re-layouts: 0.7 us -> 6.82 us
  transfers between devices with their start and end apart: 4 -> 0, of which waited for: 4 -> 0; matrix products, arithmetic and copies ran while one was open for 4% -> 0% of each run, Pallas kernels for 0% -> 0%
where the time goes in v1:
time: 37 us; the launch traced here: 36.7 us
  Pallas kernels  28.5 us (77%)
  local copies, waits for them, and re-layouts  8.2 us (22%)
    pallas_call x1, Pallas kernels, body(): pl.pallas_call(functools.partial(kernel, height, width, side_rows, sizes)...  28.5 us
    unnamed x11, local copies, waits for them, and re-layouts  6.82 us

profile of v1, /device:TPU:0, one launch (start us, length us, event | category | flops | bytes accessed | tf_op | source)
XLA Modules:
  0.0 36.7 jit_solution(7549288276277352792)
XLA Ops:
  0.0 0.7 %reshape.10.gain_s = f32[1,768]{1,0:T(1,128)S(1)} reshape(f32[768]{0:T(1024)} %param.12) | data formatting | bytes 6144 | tf_op jit(solution)/shard_map/reshape | solution.py:345
  0.7 0.7 %reshape.11.gain_t = f32[1,768]{1,0:T(1,128)S(1)} reshape(f32[768]{0:T(1024)} %param.17) | data formatting | bytes 6144 | tf_op jit(solution)/shard_map/reshape | solution.py:346
  1.4 0.0 copy-start
  1.4 1.3 %copy-done = bf16[768,768]{1,0:T(8,128)(2,1)S(1)} copy-done((bf16[768,768]{1,0:T(8,128)(2,1)S(1)}, bf16[768,768]{1,0:T(8,128)(2,1)}, u32[]{:S(2)}) %copy-start) | copy-done | bytes 1179672
  2.7 0.0 copy-start.1
  2.7 1.3 %copy-done.1 = bf16[768,768]{1,0:T(8,128)(2,1)S(1)} copy-done((bf16[768,768]{1,0:T(8,128)(2,1)S(1)}, bf16[768,768]{1,0:T(8,128)(2,1)}, u32[]{:S(2)}) %copy-start.1) | copy-done | bytes 1179672
  3.9 0.0 copy-start.2
  3.9 1.3 %copy-done.2 = bf16[768,768]{1,0:T(8,128)(2,1)S(1)} copy-done((bf16[768,768]{1,0:T(8,128)(2,1)S(1)}, bf16[768,768]{1,0:T(8,128)(2,1)}, u32[]{:S(2)}) %copy-start.2) | copy-done | bytes 1179672
  5.2 0.0 copy-start.3
  5.2 1.3 %copy-done.3 = bf16[768,768]{1,0:T(8,128)(2,1)S(1)} copy-done((bf16[768,768]{1,0:T(8,128)(2,1)S(1)}, bf16[768,768]{1,0:T(8,128)(2,1)}, u32[]{:S(2)}) %copy-start.3) | copy-done | bytes 1179672
  6.5 0.0 copy-start.4
  6.5 1.0 %copy-done.4 = bf16[4,4,16,768]{3,2,1,0:T(8,128)(2,1)S(1)} copy-done((bf16[4,4,16,768]{3,2,1,0:T(8,128)(2,1)S(1)}, bf16[4,4,16,768]{3,2,1,0:T(8,128)(2,1)}, u32[]{:S(2)}) %copy-start.4) | copy-done | bytes 393240
  7.5 28.5 %shard_map.109 = bf16[4,4,16,768]{3,2,1,0:T(8,128)(2,1)S(1)} custom-call(bf16[4,64,768]{2,1,0:T(8,128)(2,1)S(1)} %bitcast.1, f32[1,768]{1,0:T(1,128)S(1)} %reshape.10.gain_s, f32[1,768]{1,0:T(1,128)S(1)} %reshape.11.gain_t, bf16[768,768]{1,0:T(8,128)(2,1)S(1)} %copy-done, bf16[768,768]{1,0:T(8,128)(2,1)S(1)} %copy-done.1, bf16[768,768]{1,0:T(8,128)(2,1)S(1)} %copy-done.2, ...), custom_call_target="tpu_custom_call" | custom-call | flops 4227858432 | bytes 9437184 | tf_op jit(solution)/shard_map/pallas_call | solution.py:312
  35.9 0.7 %copy.13 = bf16[4,4,16,768]{3,2,1,0:T(8,128)(2,1)} copy(bf16[4,4,16,768]{3,2,1,0:T(8,128)(2,1)S(1)} %shard_map.109) | data formatting | bytes 786432
Async XLA Ops:
  1.4 1.3 %copy-start = (bf16[768,768]{1,0:T(8,128)(2,1)S(1)}, bf16[768,768]{1,0:T(8,128)(2,1)}, u32[]{:S(2)}) copy-start(bf16[768,768]{1,0:T(8,128)(2,1)} %refs_0_.1) | copy-start | bytes 3538948
  2.7 1.3 %copy-start.1 = (bf16[768,768]{1,0:T(8,128)(2,1)S(1)}, bf16[768,768]{1,0:T(8,128)(2,1)}, u32[]{:S(2)}) copy-start(bf16[768,768]{1,0:T(8,128)(2,1)} %refs_1_.1) | copy-start | bytes 3538948
  3.9 1.3 %copy-start.2 = (bf16[768,768]{1,0:T(8,128)(2,1)S(1)}, bf16[768,768]{1,0:T(8,128)(2,1)}, u32[]{:S(2)}) copy-start(bf16[768,768]{1,0:T(8,128)(2,1)} %refs_2_.1) | copy-start | bytes 3538948
  5.2 1.3 %copy-start.3 = (bf16[768,768]{1,0:T(8,128)(2,1)S(1)}, bf16[768,768]{1,0:T(8,128)(2,1)}, u32[]{:S(2)}) copy-start(bf16[768,768]{1,0:T(8,128)(2,1)} %refs_3_.1) | copy-start | bytes 3538948
  6.5 1.0 %copy-start.4 = (bf16[4,4,16,768]{3,2,1,0:T(8,128)(2,1)S(1)}, bf16[4,4,16,768]{3,2,1,0:T(8,128)(2,1)}, u32[]{:S(2)}) copy-start(bf16[4,4,16,768]{3,2,1,0:T(8,128)(2,1)} %param.11) | copy-start | bytes 1179652

commit v2 on v1

--- a/solution.py
+++ b/solution.py
@@ -59,8 +59,8 @@
 ):
     nv, nz, nx = sizes
     weights_hbm, refs = refs[:8], refs[8:]
-    out_ref, wide, sides, w, qbuf, mid, held, normed, kbuf, vbuf, back = refs[:11]
-    x_sem, w_sem, hs, hr, ms, mr, bs, br = refs[11:]
+    out_ref, wide, sides, w, qbuf, mid, held, normed, kbuf, vbuf, back, kwide, vwide = refs[:13]
+    x_sem, w_sem, hs, hr, ms, mr, bs, br = refs[13:]
     views, own, depth = x_hbm.shape
     share = own // nv
     halo = RADIUS * width
@@ -72,7 +72,7 @@
     w_copies = [
         pltpu.make_async_copy(weights_hbm[i], w.at[i], w_sem.at[i]) for i in range(8)
     ]
-    for copy in w_copies:
+    for copy in w_copies[:4]:
         copy.start()
 
     def there(dz, dx):
@@ -170,7 +170,7 @@
     )
     bias = jnp.where(seen, 0.0, very_negative).astype(jnp.float32)
     scale = HEAD_DIM ** -0.5
-    gain = gain_s[...]
+    gain = gain_s[...].reshape(1, depth)
     groups = depth // LANES
 
     own_normed = rms_norm(wide[:, pl.ds(halo, own)].reshape(views * own, depth), gain)
@@ -179,8 +179,14 @@
         (dot(own_normed, w[0]).astype(jnp.bfloat16) * scale)
         .astype(jnp.bfloat16).reshape(views, own, depth)
     )
-    for i in (1, 2, 3):
+    for copy in w_copies[4:]:
+        copy.start()
+    for i, wide_buf in ((1, kwide), (2, vwide)):
         w_copies[i].wait()
+        wide_buf[:, pl.ds(halo, own)] = (
+            dot(own_normed, w[i]).astype(jnp.bfloat16).reshape(views, own, depth)
+        )
+    w_copies[3].wait()
 
     def mid_copy(v, target, slot):
         return pltpu.make_async_remote_copy(
@@ -198,9 +204,13 @@
             def _():
                 halo_copy(k, v).wait_recv()
 
-        tokens = rms_norm(wide[v], gain)
-        keys = dot(tokens, w[1]).astype(jnp.bfloat16)
-        values = dot(tokens, w[2]).astype(jnp.bfloat16)
+        around = jnp.concatenate([wide[v, :halo], wide[v, halo + own :]], axis=0)
+        tokens = rms_norm(around, gain)
+        for i, wide_buf in ((1, kwide), (2, vwide)):
+            product = dot(tokens, w[i]).astype(jnp.bfloat16)
+            wide_buf[v, :halo] = product[:halo]
+            wide_buf[v, halo + own :] = product[halo:]
+        keys, values = kwide[v], vwide[v]
         queries = qbuf[v]
         parts = []
         for g in range(groups):
@@ -222,7 +232,7 @@
     for j in range(nv - 1):
         for v in range(views):
             mid_copy(v, peer(j), peer(j)).wait_recv()
-    tokens = rms_norm(held[...].reshape(nv * views * share, depth), gain_t[...])
+    tokens = rms_norm(held[...].reshape(nv * views * share, depth), gain_t[...].reshape(1, depth))
     normed[...] = tokens.reshape(nv, views * share, depth)
     for i in range(4, 8):
         w_copies[i].wait()
@@ -304,7 +314,7 @@
     assert own % nv == 0 and share % ROWS == 0 and width % ROWS == 0
     assert height >= RADIUS and width >= RADIUS and depth % LANES == 0
     half = jnp.bfloat16
-    hbm = pl.BlockSpec(memory_space=pl.ANY)
+    hbm = pl.BlockSpec(memory_space=pltpu.HBM)
     vmem = pl.BlockSpec(memory_space=pltpu.VMEM)
     dma = pltpu.SemaphoreType.DMA
     tokens = nv * views * share
@@ -325,6 +335,8 @@
             pltpu.VMEM((share // COLS, tokens // (share // COLS), depth), half),
             pltpu.VMEM((share // COLS, tokens // (share // COLS), depth), half),
             pltpu.VMEM((nv, views, share, depth), half),
+            pltpu.VMEM((views, wide, depth), half),
+            pltpu.VMEM((views, wide, depth), half),
             dma(()),
             dma((8,)),
             dma((len(DIRECTIONS), views)),
@@ -335,15 +347,15 @@
             dma((nv,)),
         ],
         compiler_params=pltpu.CompilerParams(
-            collective_id=0, has_side_effects=True, vmem_limit_bytes=48 * 1024 * 1024
+            collective_id=0, has_side_effects=True, vmem_limit_bytes=56 * 1024 * 1024
         ),
         cost_estimate=pl.CostEstimate(
             flops=products, bytes_accessed=16 * depth * depth, transcendentals=0
         ),
     )(
         view_maps.reshape(views, own, depth),
-        gain_spatial.reshape(1, depth),
-        gain_temporal.reshape(1, depth),
+        gain_spatial,
+        gain_temporal,
         *spatial,
         *temporal,
     )

time: 37 us -> 31.5 us (0.85)
  local copies, waits for them, and re-layouts: 8.2 us -> 1.77 us
  Pallas kernels: 28.5 us -> 29.5 us
    unnamed x11 -> x1, local copies, waits for them, and re-layouts: 6.82 us -> 1.77 us
    reshape x2 -> x0, local copies, waits for them, and re-layouts: 1.38 us -> none  [the longest x1 0.69 us: body(): gain_spatial.reshape(1, depth)]
    pallas_call x1, Pallas kernels: 28.5 us -> 29.5 us  [body(): pl.pallas_call(functools.partial(kernel, height, width, side_rows, sizes)...]
where the time goes in v2:
time: 31.5 us; the launch traced here: 31.3 us
  Pallas kernels  29.5 us (94%)
  local copies, waits for them, and re-layouts  1.77 us (6%)
    pallas_call x1, Pallas kernels, body(): pl.pallas_call(functools.partial(kernel, height, width, side_rows, sizes)...  29.5 us
    unnamed x1, local copies, waits for them, and re-layouts  1.77 us

profile of v2, /device:TPU:0, one launch (start us, length us, event | category | flops | bytes accessed | tf_op | source)
XLA Modules:
  0.0 31.3 jit_solution(4320415957596647368)
XLA Ops:
  0.0 29.5 %shard_map.109 = bf16[4,4,16,768]{3,2,1,0:T(8,128)(2,1)} custom-call(bf16[4,64,768]{2,1,0:T(8,128)(2,1)} %bitcast.1, f32[768]{0:T(1024)} %gain_s.1, f32[768]{0:T(1024)} %gain_t.1, bf16[768,768]{1,0:T(8,128)(2,1)} %refs_0_.1, bf16[768,768]{1,0:T(8,128)(2,1)} %refs_1_.1, bf16[768,768]{1,0:T(8,128)(2,1)} %refs_2_.1, bf16[768,768]{1,0:T(8,128)(2,1)} %refs_3_.1, ...), custom_call_target="tpu_custom_call" | custom-call | flops 4227858432 | bytes 9437184 | tf_op jit(solution)/shard_map/pallas_call | solution.py:322
  29.5 1.8 %copy.13 = bf16[4,4,16,768]{3,2,1,0:T(8,128)(2,1)} copy(bf16[4,4,16,768]{3,2,1,0:T(8,128)(2,1)} %shard_map.109) | data formatting | bytes 786432
